TPU v7x, 128 devices: a whole 4x4x4 slice. The times are simulated.
128 devices in a mesh: row: 8 (over z, y_hi), col: 16 (over x, y_lo, core).
Axes of the slice: x: 4, y: 4 (y_hi: 2, y_lo: 2; y = y_hi * 2 + y_lo), z: 4, core: 2. Of those that a mesh axis runs over, the one named last changes fastest.
Arguments:
- a_panels: bfloat16 [16384, 32768], P('row', 'col'), may hold values from -6 to 6
- a_flags: int32 [256, 512], P('row', 'col'), may hold values 0 or 1
- b_panels: bfloat16 [32768, 8192], P('row', 'col'), may hold values from -0.09375 to 0.09375
- b_flags: int32 [512, 128], P('row', 'col'), may hold values 0 or 1
Outputs:
- product: float32 [16384, 8192], P('row', 'col')
All inputs are finite; a program needn't handle non-finite values. No bound on the sum of `a_flags` or of `b_flags` on one device may be relied on, other than what follows from the above.
Results may differ from a plain program's by a relative error of at most 0.0003.
Values may be sent and summed in bfloat16 or wider, within the bound.
A program may use at most 128 MiB of HBM per device.

v0:
```python
import jax
import jax.numpy as jnp
from jax import lax
from jax.sharding import PartitionSpec as P

STEPS = 4


def from_behind(value, axis, steps):
    count = lax.axis_size(axis)
    pairs = [(source, (source + steps) % count) for source in range(count)]
    return lax.ppermute(value, axis, pairs)


def apply_flags(data, flags):
    blocks_down, blocks_across = flags.shape
    size = data.shape[0] // blocks_down
    shaped = data.reshape(blocks_down, size, blocks_across, size)
    masked = shaped * flags.astype(data.dtype)[:, None, :, None]
    return masked.reshape(data.shape)


def per_device(a_panels, a_flags, b_panels, b_flags):
    left = apply_flags(a_panels, a_flags)
    right = apply_flags(b_panels, b_flags)
    rows_count = lax.axis_size("row")
    cols_count = lax.axis_size("col")
    row_index = lax.axis_index("row")
    col_index = lax.axis_index("col")
    group_width = left.shape[1]
    total = jnp.zeros((left.shape[0], right.shape[1]), jnp.float32)
    left_now = left
    right_pair = right
    for step in range(STEPS):
        if step > 0:
            left_now = from_behind(left_now, "col", -1)
        if step > 0:
            right_pair = from_behind(right_pair, "row", -1)
        wanted = (row_index + col_index + step) % cols_count // rows_count
        right_now = lax.dynamic_slice_in_dim(right_pair, wanted * group_width, group_width, 0)
        total = total + jnp.dot(left_now, right_now, preferred_element_type=jnp.float32)
    return total


def solution(mesh):
    placed = (P("row", "col"), P("row", "col"), P("row", "col"), P("row", "col"))
    return jax.shard_map(
        per_device, mesh=mesh, in_specs=placed, out_specs=P("row", "col"), check_vma=False
    )
```

profile of v0, /device:TPU:1, one launch (start us, length us, event | category | flops | bytes accessed | tf_op | source)
XLA Modules:
  0.0 609.5 jit_solution(7263753143324399171)
XLA Ops:
  0.0 0.7 convert_element_type.6
  0.7 6.1 mul.34
  6.8 23.5 %mul.35 = bf16[2048,2048]{1,0:T(8,128)(2,1)} reshape(bf16[32,64,32,64]{3,2,1,0:T(8,128)(2,1)} %mul.34) | data formatting | bytes 16777216 | tf_op jit(solution)/shard_map/mul | solution.py:19
  30.3 0.0 copy-start.2
  30.3 7.5 %mul.36 = bf16[2048,2048]{1,0:T(8,128)(2,1)S(1)} multiply(bf16[2048,2048]{1,0:T(8,128)(2,1)} %param.4, bf16[2048,2048]{1,0:T(8,128)(2,1)} %mul.35) | non-fusion elementwise | flops 4194304 | bytes 25165824 | tf_op jit(solution)/shard_map/mul | solution.py:19
  37.8 0.0 copy-start
  37.8 3.2 copy-done
  41.0 1.4 collective-permute-start
  42.5 92.5 %collective-permute-done = bf16[2048,2048]{1,0:T(8,128)(2,1)} collective-permute-done((bf16[2048,2048]{1,0:T(8,128)(2,1)S(1)}, bf16[2048,2048]{1,0:T(8,128)(2,1)}, u32[]{:S(2)}, u32[]{:S(2)}) %collective-permute-start) | collective-permute-done | bytes 8388640 | tf_op jit(solution)/shard_map/ppermute | solution.py:12
  135.0 1.8 collective-permute-start.2
  136.7 0.0 copy-done.2
  136.7 0.1 copy.5
  136.8 4.4 mul.37
  141.2 11.8 %mul.38 = bf16[4096,512]{1,0:T(8,128)(2,1)} reshape(bf16[64,64,8,64]{3,2,1,0:T(8,128)(2,1)} %mul.37) | data formatting | bytes 8388608 | tf_op jit(solution)/shard_map/mul | solution.py:19
  153.0 4.7 mul.39
  157.6 0.0 copy-start.1
  157.7 2.0 copy-done.1
  159.7 6.1 collective-permute-start.1
  165.8 156.6 %collective-permute-done.1 = bf16[4096,512]{1,0:T(8,128)(2,1)} collective-permute-done((bf16[4096,512]{1,0:T(8,128)(2,1)S(1)}, bf16[4096,512]{1,0:T(8,128)(2,1)}, u32[]{:S(2)}, u32[]{:S(2)}) %collective-permute-start.1) | collective-permute-done | bytes 4194336 | tf_op jit(solution)/shard_map/ppermute | solution.py:12
  322.4 2.6 collective-permute-start.3
  325.0 0.0 collective-permute-done.2
  325.0 0.8 collective-permute-start.4
  325.8 179.9 %collective-permute-done.3 = bf16[4096,512]{1,0:T(8,128)(2,1)} collective-permute-done((bf16[4096,512]{1,0:T(8,128)(2,1)}, bf16[4096,512]{1,0:T(8,128)(2,1)}, u32[]{:S(2)}, u32[]{:S(2)}) %collective-permute-start.3) | collective-permute-done | bytes 4194336 | tf_op jit(solution)/shard_map/ppermute | solution.py:12
  505.7 4.7 collective-permute-start.5
  510.5 7.6 %fusion.5 = f32[2048,512]{1,0:T(8,128)S(1)} fusion(bf16[2048,2048]{1,0:T(8,128)(2,1)} %copy-done, bf16[4096,512]{1,0:T(8,128)(2,1)} %copy-done.1, s32[]{:T(128)S(6)} %select_n.46), kind=kOutput, calls=%fused_computation.6 | convolution fusion | flops 4294967296 | bytes 14680068 | tf_op jit(solution)/shard_map/dot_general | solution.py:41
  518.0 7.6 %fusion.3 = f32[2048,512]{1,0:T(8,128)S(1)} fusion(bf16[2048,2048]{1,0:T(8,128)(2,1)} %collective-permute-done, bf16[4096,512]{1,0:T(8,128)(2,1)} %collective-permute-done.1, s32[]{:T(128)S(6)} %select_n.49), kind=kOutput, calls=%fused_computation.4 | convolution fusion | flops 4294967296 | bytes 14680068 | tf_op jit(solution)/shard_map/dot_general | solution.py:41
  525.6 7.6 %fusion.1 = f32[2048,512]{1,0:T(8,128)S(1)} fusion(bf16[2048,2048]{1,0:T(8,128)(2,1)} %collective-permute-done.2, bf16[4096,512]{1,0:T(8,128)(2,1)} %collective-permute-done.3, s32[]{:T(128)S(6)} %select_n.52), kind=kOutput, calls=%fused_computation.2 | convolution fusion | flops 4294967296 | bytes 14680068 | tf_op jit(solution)/shard_map/dot_general | solution.py:41
  533.2 66.1 %collective-permute-done.5 = bf16[4096,512]{1,0:T(8,128)(2,1)S(1)} collective-permute-done((bf16[4096,512]{1,0:T(8,128)(2,1)}, bf16[4096,512]{1,0:T(8,128)(2,1)S(1)}, u32[]{:S(2)}, u32[]{:S(2)}) %collective-permute-start.5) | collective-permute-done | bytes 4194336 | tf_op jit(solution)/shard_map/ppermute | solution.py:12
  599.3 0.0 collective-permute-done.4
  599.3 10.2 %add_add_fusion = f32[2048,512]{1,0:T(8,128)} fusion(f32[2048,512]{1,0:T(8,128)S(1)} %fusion.1, f32[2048,512]{1,0:T(8,128)S(1)} %fusion.5, f32[2048,512]{1,0:T(8,128)S(1)} %fusion.3, bf16[2048,2048]{1,0:T(8,128)(2,1)} %collective-permute-done.4, bf16[4096,512]{1,0:T(8,128)(2,1)S(1)} %collective-permute-done.5, s32[]{:T(128)S(6)} %select_n.55), kind=kOutput, calls=%fused_computation | convolution fusion | flops 4298113024 | bytes 27262980 | tf_op jit(solution)/shard_map/dot_general | solution.py:41
  (1 shorter events, 0.0 us)
Async XLA Ops:
  30.3 106.4 %copy-start.2 = (s32[64,8]{0,1:T(8,128)S(1)}, s32[64,8]{0,1:T(8,128)}, u32[]{:S(2)}) copy-start(s32[64,8]{0,1:T(8,128)} %param.7) | copy-start | bytes 6148
  37.8 3.2 copy-start
  41.0 93.9 %collective-permute-start = (bf16[2048,2048]{1,0:T(8,128)(2,1)S(1)}, bf16[2048,2048]{1,0:T(8,128)(2,1)}, u32[]{:S(2)}, u32[]{:S(2)}) collective-permute-start(bf16[2048,2048]{1,0:T(8,128)(2,1)S(1)} %mul.36), channel_id=1, source_target_pairs={{0,15},{1,0},{2,1},{3,2},{4,3},{5,4},{6,5},{7,6},{8,7},{9,8},{10,9... | collective-permute-start | bytes 25165832 | tf_op jit(solution)/shard_map/ppermute | solution.py:12
  135.0 190.0 %collective-permute-start.2 = (bf16[2048,2048]{1,0:T(8,128)(2,1)}, bf16[2048,2048]{1,0:T(8,128)(2,1)}, u32[]{:S(2)}, u32[]{:S(2)}) collective-permute-start(bf16[2048,2048]{1,0:T(8,128)(2,1)} %collective-permute-done), channel_id=1, source_target_pairs={{0,15},{1,0},{2,1},{3,2},{4,3},{5,4},{6,5},{7,6},{8,7},{9,8},{10,9... | collective-permute-start | bytes 25165832 | tf_op jit(solution)/shard_map/ppermute | solution.py:12
  157.6 2.0 copy-start.1
  159.7 162.7 %collective-permute-start.1 = (bf16[4096,512]{1,0:T(8,128)(2,1)S(1)}, bf16[4096,512]{1,0:T(8,128)(2,1)}, u32[]{:S(2)}, u32[]{:S(2)}) collective-permute-start(bf16[4096,512]{1,0:T(8,128)(2,1)S(1)} %mul.39), channel_id=1, source_target_pairs={{0,112},{16,0},{32,16},{48,32},{64,48},{80,64},{96,80},{112,96},{1... | collective-permute-start | bytes 12582920 | tf_op jit(solution)/shard_map/ppermute | solution.py:12
  322.4 183.4 %collective-permute-start.3 = (bf16[4096,512]{1,0:T(8,128)(2,1)}, bf16[4096,512]{1,0:T(8,128)(2,1)}, u32[]{:S(2)}, u32[]{:S(2)}) collective-permute-start(bf16[4096,512]{1,0:T(8,128)(2,1)} %collective-permute-done.1), channel_id=1, source_target_pairs={{0,112},{16,0},{32,16},{48,32},{64,48},{80,64},{96,80},{112,96},{1... | collective-permute-start | bytes 12582920 | tf_op jit(solution)/shard_map/ppermute | solution.py:12
  325.0 274.3 %collective-permute-start.4 = (bf16[2048,2048]{1,0:T(8,128)(2,1)}, bf16[2048,2048]{1,0:T(8,128)(2,1)}, u32[]{:S(2)}, u32[]{:S(2)}) collective-permute-start(bf16[2048,2048]{1,0:T(8,128)(2,1)} %collective-permute-done.2), channel_id=1, source_target_pairs={{0,15},{1,0},{2,1},{3,2},{4,3},{5,4},{6,5},{7,6},{8,7},{9,8},{10,9... | collective-permute-start | bytes 25165832 | tf_op jit(solution)/shard_map/ppermute | solution.py:12
  505.7 93.6 %collective-permute-start.5 = (bf16[4096,512]{1,0:T(8,128)(2,1)}, bf16[4096,512]{1,0:T(8,128)(2,1)S(1)}, u32[]{:S(2)}, u32[]{:S(2)}) collective-permute-start(bf16[4096,512]{1,0:T(8,128)(2,1)} %collective-permute-done.3), channel_id=1, source_target_pairs={{0,112},{16,0},{32,16},{48,32},{64,48},{80,64},{96,80},{112,96},{1... | collective-permute-start | bytes 12582920 | tf_op jit(solution)/shard_map/ppermute | solution.py:12
where the time goes:
time: 613 us; the launch traced here: 609 us
  waiting for transfers between devices  495 us (81%)
  local copies, waits for them, and re-layouts  51 us (8%)
  matrix products  32.9 us (5%)
  starting transfers between devices  17.4 us (3%)
  other arithmetic  12.9 us (2%)
    ppermute x6, waiting for transfers between devices, from_behind(): return lax.ppermute(value, axis, pairs)  495 us
    mul x4, local copies, waits for them, and re-layouts, apply_flags(): masked = shaped * flags.astype(data.dtype)[:, None, :, None]  45.7 us
    dot_general x4, matrix products, per_device(): jnp.dot(left_now, right_now, preferred_element_type=jnp.float32)  32.9 us
    ppermute x6, starting transfers between devices, from_behind(): return lax.ppermute(value, axis, pairs)  17.4 us
  transfers between devices with their start and end apart: 6, of which 4 were waited for; matrix products, arithmetic and copies ran while one was open for 7% of the time, Pallas kernels for 0%

commit v1 on v0

v1 whole, which is shorter than its diff:
```python
import functools

import jax
import jax.numpy as jnp
from jax import lax
from jax.experimental import pallas as pl
from jax.experimental.pallas import tpu as pltpu
from jax.sharding import PartitionSpec as P

MESH = pl.DeviceIdType.MESH
TILE = 256
HALF = 256
PAD = 16
FINE = 64.0


def lanes_expanded(flags, width):
    count = flags.shape[1]
    owner = lax.broadcasted_iota(jnp.int32, (count, width), 1) // (width // count)
    spread = (owner == lax.broadcasted_iota(jnp.int32, (count, width), 0)).astype(jnp.float32)
    return jnp.dot(flags.astype(jnp.float32), spread, preferred_element_type=jnp.float32)


def coded(value, out_ref):
    rows = value.shape[0]
    largest = jnp.maximum(jnp.max(jnp.abs(value), axis=0, keepdims=True), 1e-30)
    power = jnp.ceil(jnp.log2(largest) * FINE + 0.5)
    scaled = value * (jnp.exp2(power * (-1.0 / FINE)) * 32767.0)
    whole = jnp.round(jnp.clip(scaled, -32767.0, 32767.0))
    out_ref[pl.ds(0, rows), :] = whole.astype(jnp.int32).astype(jnp.int16)
    out_ref[pl.ds(rows, PAD), :] = jnp.broadcast_to(power.astype(jnp.int32), (PAD, value.shape[1])).astype(jnp.int16)


def decoded(in_ref, rows):
    power = in_ref[pl.ds(rows, PAD), :].astype(jnp.int32).astype(jnp.float32)[0:1, :]
    scale = jnp.exp2(power * (1.0 / FINE)) * (1.0 / 32767.0)
    return in_ref[pl.ds(0, rows), :].astype(jnp.int32).astype(jnp.float32) * scale


def kernel(
    n_row, n_col, a_ref, af_ref, b_ref, bf_ref, o_ref,
    left, right, fa, fb, rx, ry, rz, acc, xs, xr, qs, qr, zs, zr,
    a_sem, b_sem, o_sem, send_r, recv_rx, recv_ry, recv_rz,
    send_x, recv_x, send_q, recv_q, send_z, recv_z,
):
    i, j = lax.axis_index("row"), lax.axis_index("col")
    even = lax.rem(j, 2) == 0
    rows, depth = left.shape
    halves, tiles = ry.shape[0], rows // TILE

    def at(di, dj):
        return (lax.rem(i + di + n_row, n_row), lax.rem(j + dj + n_col, n_col))

    def either(e, o):
        return tuple(jnp.where(even, p, q) for p, q in zip(e, o, strict=True))

    def load_a(m):
        part = pl.ds(m * TILE, TILE)
        return pltpu.make_async_copy(a_ref.at[part, :], left.at[part, :], a_sem.at[m])

    def load_b(n):
        return pltpu.make_async_copy(b_ref.at[:, pl.ds(n * HALF, HALF)], right.at[n], b_sem.at[n])

    for n in range(halves):
        load_b(n).start()
    for m in range(tiles):
        load_a(m).start()

    barrier = pltpu.get_barrier_semaphore()

    def greet(where):
        pl.semaphore_signal(barrier, inc=1, device_id=where, device_id_type=MESH)

    greet(either(at(1, -1), at(3, -3)))
    greet(at(2, -2))
    greet(at(0, 2))
    greet(either(at(0, 1), at(0, -1)))

    @pl.when(jnp.logical_not(even))
    def _():
        greet(at(0, 3))

        @pl.when(i != 0)
        def _():
            greet(at(-1, 1))

        @pl.when(i == 0)
        def _():
            greet(at(1, -1))

    @pl.when(jnp.logical_and(even, i == n_row - 1))
    def _():
        greet(at(3, -3))

    fb[...] = lanes_expanded(bf_ref[...], fb.shape[1])
    size_b = b_ref.shape[0] // fb.shape[0]
    fa[...] = lanes_expanded(af_ref[...], depth)
    size_a = rows // fa.shape[0]

    def mask_b(n):
        @pl.loop(0, fb.shape[0])
        def _(k):
            part = pl.ds(pl.multiple_of(k * size_b, size_b), size_b)
            row = fb[pl.ds(k, 1), pl.ds(n * HALF, HALF)].astype(jnp.bfloat16)
            right[n, part, :] = right[n, part, :] * row

    own = lax.rem(i + j, n_col) // n_row

    def half_for(s):
        return lax.rem(own + jnp.where(i < s, 1, 0), 2)

    def block(n, half):
        return right.at[n, pl.ds(pl.multiple_of(half * depth, depth), depth), :]

    def remote(src, dst, ssem, rsem, where):
        return pltpu.make_async_remote_copy(
            src_ref=src, dst_ref=dst, send_sem=ssem, recv_sem=rsem, device_id=where, device_id_type=MESH
        )

    to_x = either(at(-3, 3), at(-1, 1))
    to_y = at(-2, 2)
    to_forward = either(at(1, -1), at(-1, 1))
    to_extra = either(at(-1, 1), at(-3, 3))
    forwards = jnp.where(even, i != n_row - 1, i != 0)
    extra = jnp.where(even, i == 1, i == 2)

    def send_x_block(n):
        half = jnp.where(even, half_for(3), half_for(1))
        return remote(block(n, half), rx.at[n], send_r.at[0, n], recv_rx.at[n], to_x)

    def send_y_block(n):
        return remote(block(n, half_for(2)), ry.at[n], send_r.at[1, n], recv_ry.at[n], to_y)

    def send_extra(n):
        half = jnp.where(even, half_for(1), half_for(3))
        return remote(block(n, half), rz.at[n], send_r.at[3, n], recv_rz.at[n], to_extra)

    def send_forward(n):
        return remote(ry.at[n], rz.at[n], send_r.at[2, n], recv_rz.at[n], to_forward)

    def begin(n):
        send_y_block(n).start()
        send_x_block(n).start()

        @pl.when(extra)
        def _():
            send_extra(n).start()

    load_b(0).wait()
    mask_b(0)
    pl.semaphore_wait(
        barrier, jnp.where(even, 6 + jnp.where(i == 1, 1, 0) - jnp.where(i == n_row - 1, 1, 0), 4 + jnp.where(i == 2, 1, 0))
    )
    begin(0)
    load_b(1).wait()
    mask_b(1)

    @pl.loop(0, tiles)
    def _(m):
        load_a(m).wait()
        for k in range(TILE // size_a):
            part = pl.ds(pl.multiple_of(m * TILE + k * size_a, size_a), size_a)
            row = fa[pl.ds(m * (TILE // size_a) + k, 1), :].astype(jnp.bfloat16)
            left[part, :] = left[part, :] * row

    def product(m, block_ref):
        part = pl.ds(pl.multiple_of(m * TILE, TILE), TILE)
        return jnp.dot(left[part, :], block_ref[...], preferred_element_type=jnp.float32)

    for n in range(halves):
        @pl.loop(0, tiles)
        def _(m):
            acc[n, m] = product(m, block(n, own))

    send_y_block(0).wait_send()
    send_x_block(0).wait_send()
    begin(1)

    partner = either(at(0, 1), at(0, -1))

    def x_copy(n, m):
        return remote(xs.at[n, m], xr.at[n, m], send_x.at[n, m], recv_x.at[n, m], partner)

    def q_copy(n, m):
        return remote(qs.at[n, m], qr.at[n, m], send_q.at[n, m], recv_q.at[n, m], at(0, -2))

    def z_copy(n, m):
        return remote(zs.at[n, m], zr.at[n, m], send_z.at[n, m], recv_z.at[n, m], either(at(0, -3), at(0, -1)))

    for n in range(halves):
        send_y_block(n).wait_recv()

        @pl.when(forwards)
        def _():
            send_forward(n).start()

        send_x_block(n).wait_recv()

        @pl.loop(0, tiles)
        def _(m):
            xs[n, m] = product(m, rx.at[n])
            x_copy(n, m).start()

        @pl.loop(0, tiles)
        def _(m):
            value = product(m, ry.at[n])
            x_copy(n, m).wait_recv()
            coded(value + xr[n, m], qs.at[n, m])
            q_copy(n, m).start()

    for n in range(halves):
        send_forward(n).wait_recv()

        @pl.loop(0, tiles)
        def _(m):
            coded(product(m, rz.at[n]), zs.at[n, m])
            z_copy(n, m).start()

    def store(n, m):
        where = o_ref.at[pl.ds(pl.multiple_of(m * TILE, TILE), TILE), pl.ds(n * HALF, HALF)]
        return pltpu.make_async_copy(acc.at[n, m], where, o_sem.at[n, m])

    for n in range(halves):
        @pl.loop(0, tiles)
        def _(m):
            q_copy(n, m).wait_recv()
            z_copy(n, m).wait_recv()
            acc[n, m] = acc[n, m] + decoded(qr.at[n, m], TILE) + decoded(zr.at[n, m], TILE)
            store(n, m).start()

    for n in range(halves):
        if n > 0:
            send_y_block(n).wait_send()
            send_x_block(n).wait_send()

        @pl.when(forwards)
        def _():
            send_forward(n).wait_send()

        @pl.when(extra)
        def _():
            send_extra(n).wait_send()

        @pl.loop(0, tiles)
        def _(m):
            x_copy(n, m).wait_send()
            q_copy(n, m).wait_send()
            z_copy(n, m).wait_send()
            store(n, m).wait()


def per_device(n_row, n_col, a_panels, a_flags, b_panels, b_flags):
    rows, depth = a_panels.shape
    columns = b_panels.shape[1]
    halves, tiles = columns // HALF, rows // TILE
    bf16, f32, dma = jnp.bfloat16, jnp.float32, pltpu.SemaphoreType.DMA
    taken = pltpu.VMEM((halves, depth, HALF), bf16)
    tile = pltpu.VMEM((halves, tiles, TILE, HALF), f32)
    code = pltpu.VMEM((halves, tiles, TILE + PAD, HALF), jnp.int16)
    each = dma((halves, tiles))
    return pl.pallas_call(
        functools.partial(kernel, n_row, n_col),
        name="block_products",
        out_shape=jax.ShapeDtypeStruct((rows, columns), f32),
        in_specs=[
            pl.BlockSpec(memory_space=pl.ANY),
            pl.BlockSpec(memory_space=pltpu.VMEM),
            pl.BlockSpec(memory_space=pl.ANY),
            pl.BlockSpec(memory_space=pltpu.VMEM),
        ],
        out_specs=pl.BlockSpec(memory_space=pl.ANY),
        scratch_shapes=[
            pltpu.VMEM((rows, depth), bf16),
            pltpu.VMEM((halves, b_panels.shape[0], HALF), bf16),
            pltpu.VMEM((a_flags.shape[0], depth), f32),
            pltpu.VMEM((b_flags.shape[0], columns), f32),
            taken, taken, taken,
            tile, tile, tile,
            code, code, code, code,
            dma((tiles,)), dma((halves,)), each,
            dma((4, halves)), dma((halves,)), dma((halves,)), dma((halves,)),
            each, each, each, each, each, each,
        ],
        compiler_params=pltpu.CompilerParams(
            collective_id=0, has_side_effects=True, vmem_limit_bytes=60 * 2**20
        ),
        cost_estimate=pl.CostEstimate(
            flops=8 * rows * depth * columns, bytes_accessed=2 * rows * depth + 8 * rows * columns, transcendentals=0
        ),
    )(a_panels, a_flags, b_panels, b_flags)


def solution(mesh):
    placed = (P("row", "col"), P("row", "col"), P("row", "col"), P("row", "col"))
    return jax.shard_map(
        functools.partial(per_device, mesh.shape["row"], mesh.shape["col"]),
        mesh=mesh, in_specs=placed, out_specs=P("row", "col"), check_vma=False,
    )
```

time: 613 us -> 215 us (0.35)
  waiting for transfers between devices: 495 us -> 0 us
  Pallas kernels: 0 us -> 206 us
  local copies, waits for them, and re-layouts: 51 us -> 6.02 us
  matrix products: 32.9 us -> 0 us
  starting transfers between devices: 17.4 us -> 0 us
  other arithmetic: 12.9 us -> 0 us
    ppermute x6 -> x0, waiting for transfers between devices: 495 us -> none  [from_behind(): return lax.ppermute(value, axis, pairs)]
    pallas_call x0 -> x1, Pallas kernels: none -> 206 us  [per_device(): pl.pallas_call(functools.partial(kernel, n_row, n_col), name='block_produ...]
    mul x4 -> x0, local copies, waits for them, and re-layouts: 45.7 us -> none  [apply_flags(): masked = shaped * flags.astype(data.dtype)[:, None, :, None]]
    dot_general x4 -> x0, matrix products: 32.9 us -> none  [per_device(): jnp.dot(left_now, right_now, preferred_element_type=jnp.float32)]
    ppermute x6 -> x0, starting transfers between devices: 17.4 us -> none  [from_behind(): return lax.ppermute(value, axis, pairs)]
    mul x2 -> x0, other arithmetic: 12.2 us -> none  [apply_flags(): masked = shaped * flags.astype(data.dtype)[:, None, :, None]]
  transfers between devices with their start and end apart: 6 -> 0, of which waited for: 4 -> 0; matrix products, arithmetic and copies ran while one was open for 7% -> 0% of each run, Pallas kernels for 0% -> 0%
where the time goes in v1:
time: 215 us; the launch traced here: 212 us
  Pallas kernels  206 us (96%)
  local copies, waits for them, and re-layouts  6.02 us (3%)
    pallas_call x1, Pallas kernels, per_device(): pl.pallas_call(functools.partial(kernel, n_row, n_col), name='block_produ...  206 us
    unnamed x2, local copies, waits for them, and re-layouts  6.02 us

profile of v1, /device:TPU:1, one launch (start us, length us, event | category | flops | bytes accessed | tf_op | source)
XLA Modules:
  0.0 212.5 jit_solution(15664004908383218193)
XLA Ops:
  0.0 1.4 copy.5.bf_ref
  1.4 206.4 %block_products.1 = f32[2048,512]{1,0:T(8,128)} custom-call(bf16[2048,2048]{1,0:T(8,128)(2,1)} %a_ref.1, s32[32,32]{1,0:T(8,128)} %af_ref.1, bf16[4096,512]{1,0:T(8,128)(2,1)} %b_ref.1, s32[64,8]{1,0:T(8,128)} %copy.5.bf_ref), custom_call_target="tpu_custom_call" | custom-call | flops 17179869184 | bytes 16777216 | tf_op jit(solution)/shard_map/block_products/pallas_call | solution.py:261
  207.8 4.6 %copy.7 = f32[2048,512]{1,0:T(8,128)} copy(f32[2048,512]{1,0:T(8,128)} %block_products.1) | data formatting | bytes 8388608

commit v2 on v1

v2 whole, which is shorter than its diff:
```python
import functools

import jax
import jax.numpy as jnp
from jax import lax
from jax.experimental import pallas as pl
from jax.experimental.pallas import tpu as pltpu
from jax.sharding import PartitionSpec as P

MESH = pl.DeviceIdType.MESH
TILE = 512
GROUP = 256
CHUNK = 128
PAD = 16
FINE = 64.0
PIECES = 4
AHEAD = 2
FIRST, END, SECOND = 1, 2, 3

def lanes_expanded(flags, width, across=1):
    count = flags.shape[across]
    owner = lax.broadcasted_iota(jnp.int32, (count, width), 1) // (width // count)
    spread = (owner == lax.broadcasted_iota(jnp.int32, (count, width), 0)).astype(jnp.float32)
    return lax.dot_general(flags.astype(jnp.float32), spread, (((across,), (0,)), ((), ())), preferred_element_type=jnp.float32)


def coded(value, out_ref):
    for g in range(value.shape[0] // GROUP):
        part = value[g * GROUP : (g + 1) * GROUP]
        largest = jnp.maximum(jnp.max(jnp.abs(part), axis=0, keepdims=True), 1e-30)
        power = jnp.ceil(jnp.log2(largest) * FINE + 0.5)
        scaled = part * (jnp.exp2(power * (-1.0 / FINE)) * 32767.0)
        whole = jnp.round(jnp.clip(scaled, -32767.0, 32767.0))
        start = g * (GROUP + PAD)
        out_ref[pl.ds(start, GROUP), :] = whole.astype(jnp.int32).astype(jnp.int16)
        shown = jnp.broadcast_to(power.astype(jnp.int32), (PAD, part.shape[1]))
        out_ref[pl.ds(start + GROUP, PAD), :] = shown.astype(jnp.int16)


def decoded(in_ref, g):
    start = g * (GROUP + PAD)
    power = in_ref[pl.ds(start + GROUP, PAD), :].astype(jnp.int32).astype(jnp.float32)[0:1, :]
    scale = jnp.exp2(power * (1.0 / FINE)) * (1.0 / 32767.0)
    return in_ref[pl.ds(start, GROUP), :].astype(jnp.int32).astype(jnp.float32) * scale


def kernel(
    n_row, n_col, a_ref, af_ref, b_ref, bf_ref, o_ref,
    left, right, fa, fb, held, relay, spare, kept, acc, xs, xr, qs, qr, zs, zr,
    a_sem, b_sem, own_sem, o_sem, send_r, recv_r,
    send_x, recv_x, send_q, recv_q, send_z, recv_z,
):
    i, j = lax.axis_index("row"), lax.axis_index("col")
    even = lax.rem(j, 2) == 0
    other = jnp.logical_not(even)
    side = lax.rem(j // 2, 2)
    rows, depth = left.shape
    chunks, tiles = held.shape[0], rows // TILE
    part_depth = depth // PIECES

    def at(di, dj):
        return (lax.rem(i + di + n_row, n_row), lax.rem(j + dj + n_col, n_col))

    def either(e, o):
        return tuple(jnp.where(even, p, q) for p, q in zip(e, o, strict=True))

    def load_a(m):
        part = pl.ds(pl.multiple_of(m * TILE, TILE), TILE)
        return pltpu.make_async_copy(a_ref.at[part, :], left.at[part, :], a_sem.at[m])

    def load_b(n):
        return pltpu.make_async_copy(b_ref.at[:, pl.ds(n * CHUNK, CHUNK)], right.at[n], b_sem.at[n])

    load_b(0).start()

    barrier = pltpu.get_barrier_semaphore()
    near = [(-2, 4 * side), (2, -4 * side), (-2, 0), (2, 0), (4, 0), (-1, 3), (-1, -1), (1, -3), (1, 1), (1, -1), (-1, 1)]
    near += [(0, d) for d in (-3, -2, -1, 1, 2, 3)]
    for di, dj in near:
        pl.semaphore_signal(barrier, inc=1, device_id=at(di, dj), device_id_type=MESH)

    fb[...] = lanes_expanded(bf_ref[...], fb.shape[1], 0)
    size_b = b_ref.shape[0] // fb.shape[0]

    def mask_b(n):
        @pl.loop(0, fb.shape[0] // 8)
        def _(k):
            flags = fb[pl.ds(pl.multiple_of(k * 8, 8), 8), pl.ds(n * CHUNK, CHUNK)]
            for r in range(8):
                part = pl.ds(pl.multiple_of((k * 8 + r) * size_b, size_b), size_b)
                right[n, part, :] = right[n, part, :] * flags[r : r + 1].astype(jnp.bfloat16)

    own = lax.rem(i + j, n_col) // n_row

    def half_for(s):
        return lax.rem(own + jnp.where(i < s, 1, 0), 2)

    def block(n, half):
        return right.at[n, pl.ds(pl.multiple_of(half * depth, depth), depth), :]

    def piece(n, u, half):
        start = pl.multiple_of(half * depth + u * part_depth, part_depth)
        return right.at[n, pl.ds(start, part_depth), :]

    def place(n, u, slot):
        return held.at[n, pl.ds(u * part_depth, part_depth), pl.ds(slot * CHUNK, CHUNK)]

    def passing(n, u):
        return relay.at[n, pl.ds(u * part_depth, part_depth), :]

    def passing_too(n, u):
        return spare.at[n, pl.ds(u * part_depth, part_depth), :]

    def remote(src, dst, ssem, rsem, where):
        return pltpu.make_async_remote_copy(
            src_ref=src, dst_ref=dst, send_sem=ssem, recv_sem=rsem, device_id=where, device_id_type=MESH
        )

    OWN, Z, X, Y, VIA, TOO, EXTRA = range(7)

    def send_via(n, u):
        return remote(
            piece(n, u, half_for(2)), passing(n, u), send_r.at[VIA, n, u], recv_r.at[VIA, n, u], at(-2, 4 * side)
        )

    def hand_y(n, u):
        return remote(
            passing(n, u), place(n, u, Y), send_r.at[Y, n, u], recv_r.at[Y, n, u], at(0, 2 - 4 * side)
        )

    def hand_x(n, u):
        to = either(at(-1, 3 - 4 * side), at(1, 1 - 4 * side))
        return remote(passing(n, u), place(n, u, X), send_r.at[X, n, u], recv_r.at[X, n, u], to)

    def hand_z(n, u):
        to = either(at(1, -1), at(-1, 1))
        return remote(place(n, u, Y), place(n, u, Z), send_r.at[Z, n, u], recv_r.at[Z, n, u], to)

    def send_too(n, u):
        first = i == 1
        half = jnp.where(first, half_for(1), half_for(3))
        across = jnp.where(even, 4 * side, 0)
        to = tuple(jnp.where(first, p, q) for p, q in zip(at(4, 0), at(-2, across), strict=True))
        return remote(piece(n, u, half), passing_too(n, u), send_r.at[TOO, n, u], recv_r.at[TOO, n, u], to)

    def pass_too(n, u):
        return remote(passing_too(n, u), passing_too(n, u), send_r.at[EXTRA, n, u], recv_r.at[TOO, n, u], at(2, 0))

    def hand_too(n, u, slot):
        first = i == n_row - 1
        back = at(-1, 3 - jnp.where(even, 4 * side, 0))
        to = tuple(jnp.where(first, p, q) for p, q in zip(at(1, 1), back, strict=True))
        return remote(passing_too(n, u), place(n, u, slot), send_r.at[EXTRA, n, u], recv_r.at[slot, n, u], to)

    gives_x = jnp.where(even, i != 0, i != n_row - 1)
    gives_z = jnp.where(even, i != n_row - 1, i != 0)
    sends_too = jnp.logical_or(i == 1, i == 2)
    passes_too = jnp.logical_or(i == 5, jnp.logical_or(i == 0, i == n_row - 1))

    def begin(n, u):
        send_via(n, u).start()

        @pl.when(sends_too)
        def _():
            send_too(n, u).start()

    def hand_on(n, u):
        send_via(n, u).wait_recv()
        hand_y(n, u).start()

        @pl.when(gives_x)
        def _():
            hand_x(n, u).start()

        @pl.when(i == 5)
        def _():
            send_too(n, u).wait_recv()
            pass_too(n, u).start()

        @pl.when(i == 0)
        def _():
            send_too(n, u).wait_recv()

        @pl.when(jnp.logical_and(even, i == 0))
        def _():
            hand_too(n, u, X).start()

        @pl.when(jnp.logical_and(other, i == 0))
        def _():
            hand_too(n, u, Z).start()

    def hand_third(n, u):
        hand_y(n, u).wait_recv()

        @pl.when(gives_z)
        def _():
            hand_z(n, u).start()

        @pl.when(i == n_row - 1)
        def _():
            send_too(n, u).wait_recv()

        @pl.when(jnp.logical_and(even, i == n_row - 1))
        def _():
            hand_too(n, u, Z).start()

        @pl.when(jnp.logical_and(other, i == n_row - 1))
        def _():
            hand_too(n, u, X).start()

    def own_copy(n):
        return pltpu.make_async_copy(block(n, own), held.at[n, :, pl.ds(0, CHUNK)], own_sem.at[n])

    load_b(0).wait()
    for n in range(1, chunks):
        load_b(n).start()
    for m in range(tiles):
        load_a(m).start()
    mask_b(0)
    pl.semaphore_wait(barrier, len(near))
    for u in range(AHEAD):
        begin(0, u)
    own_copy(0).start()
    for n in range(1, chunks):
        load_b(n).wait()
        mask_b(n)
        own_copy(n).start()

    fa[...] = lanes_expanded(af_ref[...], depth)
    size_a = rows // fa.shape[0]

    @pl.loop(0, tiles)
    def _(m):
        load_a(m).wait()

        @pl.loop(0, TILE // size_a)
        def _(k):
            part = pl.ds(pl.multiple_of(m * TILE + k * size_a, size_a), size_a)
            row = fa[pl.ds(m * (TILE // size_a) + k, 1), :].astype(jnp.bfloat16)
            left[part, :] = left[part, :] * row

    for n in range(chunks):
        own_copy(n).wait()

    partner = either(at(0, 1), at(0, -1))

    def x_copy(n, m):
        return remote(xs.at[n, m], xr.at[n, m], send_x.at[n, m], recv_x.at[n, m], partner)

    def q_copy(n, m):
        return remote(qs.at[n, m], qr.at[n, m], send_q.at[n, m], recv_q.at[n, m], at(0, -2))

    def z_copy(n, m):
        return remote(zs.at[n, m], zr.at[n, m], send_z.at[n, m], recv_z.at[n, m], either(at(0, -3), at(0, -1)))

    def product(n, m, first):
        part = pl.ds(pl.multiple_of(m * TILE, TILE), TILE)
        pair = held[n, :, first * CHUNK : (first + 2) * CHUNK]
        return jnp.dot(left[part, :], pair, preferred_element_type=jnp.float32)

    def first_pair(n):
        for u in range(PIECES):
            hand_x(n, u).wait_recv()

        @pl.loop(0, tiles)
        def _(m):
            value = product(n, m, X)
            xs[n, m] = value[:, :CHUNK]
            x_copy(n, m).start()
            kept[m] = value[:, CHUNK:]

    def first_end(n):
        @pl.loop(0, tiles)
        def _(m):
            x_copy(n, m).wait_recv()
            coded(kept[m] + xr[n, m], qs.at[n, m])
            q_copy(n, m).start()

    def second_pair(n):
        for u in range(PIECES):
            hand_z(n, u).wait_recv()

        @pl.loop(0, tiles)
        def _(m):
            value = product(n, m, OWN)
            acc[n, m] = value[:, :CHUNK]
            coded(value[:, CHUNK:], zs.at[n, m])
            z_copy(n, m).start()

    @pl.loop(0, chunks)
    def _(n):
        for u in range(PIECES):
            ahead, rest = divmod(u + AHEAD, PIECES)

            @pl.when(n + ahead < chunks)
            def _():
                begin(n + ahead, rest)

            hand_on(n, u)
            if u == 0:
                @pl.when(n > 0)
                def _():
                    hand_third(n - 1, PIECES - 1)
            else:
                hand_third(n, u - 1)
            if u == FIRST:
                @pl.when(n > 0)
                def _():
                    first_pair(n - 1)
            if u == END:
                @pl.when(n > 0)
                def _():
                    first_end(n - 1)
            if u == SECOND:
                @pl.when(n > 0)
                def _():
                    second_pair(n - 1)

    hand_third(chunks - 1, PIECES - 1)
    first_pair(chunks - 1)
    first_end(chunks - 1)
    second_pair(chunks - 1)

    def store(n, m):
        where = o_ref.at[
            pl.ds(pl.multiple_of(m * TILE, TILE), TILE), pl.ds(pl.multiple_of(n * CHUNK, CHUNK), CHUNK)
        ]
        return pltpu.make_async_copy(acc.at[n, m], where, o_sem.at[n, m])

    @pl.loop(0, chunks)
    def _(n):
        @pl.loop(0, tiles)
        def _(m):
            q_copy(n, m).wait_recv()
            z_copy(n, m).wait_recv()
            for g in range(TILE // GROUP):
                part = pl.ds(g * GROUP, GROUP)
                acc[n, m, part, :] = acc[n, m, part, :] + decoded(qr.at[n, m], g) + decoded(zr.at[n, m], g)
            store(n, m).start()

    @pl.loop(0, chunks)
    def _(n):
        for u in range(PIECES):
            send_via(n, u).wait_send()
            hand_y(n, u).wait_send()

            @pl.when(gives_x)
            def _():
                hand_x(n, u).wait_send()

            @pl.when(gives_z)
            def _():
                hand_z(n, u).wait_send()

            @pl.when(sends_too)
            def _():
                send_too(n, u).wait_send()

            @pl.when(passes_too)
            def _():
                pass_too(n, u).wait_send()

        @pl.loop(0, tiles)
        def _(m):
            x_copy(n, m).wait_send()
            q_copy(n, m).wait_send()
            z_copy(n, m).wait_send()
            store(n, m).wait()


def per_device(n_row, n_col, a_panels, a_flags, b_panels, b_flags):
    rows, depth = a_panels.shape
    columns = b_panels.shape[1]
    chunks, tiles = columns // CHUNK, rows // TILE
    bf16, f32, dma = jnp.bfloat16, jnp.float32, pltpu.SemaphoreType.DMA
    tile = pltpu.VMEM((chunks, tiles, TILE, CHUNK), f32)
    code = pltpu.VMEM((chunks, tiles, TILE // GROUP * (GROUP + PAD), CHUNK), jnp.int16)
    each = dma((chunks, tiles))
    return pl.pallas_call(
        functools.partial(kernel, n_row, n_col),
        name="block_products",
        out_shape=jax.ShapeDtypeStruct((rows, columns), f32),
        in_specs=[
            pl.BlockSpec(memory_space=pl.ANY),
            pl.BlockSpec(memory_space=pltpu.VMEM),
            pl.BlockSpec(memory_space=pl.ANY),
            pl.BlockSpec(memory_space=pltpu.VMEM),
        ],
        out_specs=pl.BlockSpec(memory_space=pl.ANY),
        scratch_shapes=[
            pltpu.VMEM((rows, depth), bf16),
            pltpu.VMEM((chunks, b_panels.shape[0], CHUNK), bf16),
            pltpu.VMEM((a_flags.shape[0], depth), f32),
            pltpu.VMEM((b_flags.shape[0], columns), f32),
            pltpu.VMEM((chunks, depth, 4 * CHUNK), bf16),
            pltpu.VMEM((chunks, depth, CHUNK), bf16),
            pltpu.VMEM((chunks, depth, CHUNK), bf16),
            pltpu.VMEM((tiles, TILE, CHUNK), f32),
            tile, tile, tile,
            code, code, code, code,
            dma((tiles,)), dma((chunks,)), dma((chunks,)), each,
            dma((7, chunks, PIECES)), dma((6, chunks, PIECES)),
            each, each, each, each, each, each,
        ],
        compiler_params=pltpu.CompilerParams(
            collective_id=0, has_side_effects=True, vmem_limit_bytes=60 * 2**20
        ),
        cost_estimate=pl.CostEstimate(
            flops=8 * rows * depth * columns, bytes_accessed=2 * rows * depth + 8 * rows * columns, transcendentals=0
        ),
    )(a_panels, a_flags, b_panels, b_flags.T)


def solution(mesh):
    placed = (P("row", "col"), P("row", "col"), P("row", "col"), P("row", "col"))
    return jax.shard_map(
        functools.partial(per_device, mesh.shape["row"], mesh.shape["col"]),
        mesh=mesh, in_specs=placed, out_specs=P("row", "col"), check_vma=False,
    )
```

time: 215 us -> 167 us (0.78); the launches traced: 212 us -> 167 us
  Pallas kernels: 206 us -> 162 us
    pallas_call x1, Pallas kernels: 206 us -> 162 us  [per_device(): pl.pallas_call(functools.partial(kernel, n_row, n_col), name='block_produ...]
    unnamed x2 -> x1, local copies, waits for them, and re-layouts: 6.02 us -> 4.64 us
where the time goes in v2:
time: 167 us
  Pallas kernels  162 us (97%)
  local copies, waits for them, and re-layouts  4.64 us (3%)
    pallas_call x1, Pallas kernels, per_device(): pl.pallas_call(functools.partial(kernel, n_row, n_col), name='block_produ...  162 us
    unnamed x1, local copies, waits for them, and re-layouts  4.64 us

profile of v2, /device:TPU:1, one launch (start us, length us, event | category | flops | bytes accessed | tf_op | source)
XLA Modules:
  0.0 167.1 jit_solution(5035178464725156900)
XLA Ops:
  0.0 162.5 %block_products.1 = f32[2048,512]{1,0:T(8,128)} custom-call(bf16[2048,2048]{1,0:T(8,128)(2,1)} %a_ref.1, s32[32,32]{1,0:T(8,128)} %af_ref.1, bf16[4096,512]{1,0:T(8,128)(2,1)} %b_ref.1, s32[8,64]{1,0:T(8,128)} %bitcast.1), custom_call_target="tpu_custom_call" | custom-call | flops 17179869184 | bytes 16777216 | tf_op jit(solution)/shard_map/block_products/pallas_call | solution.py:379
  162.5 4.6 %copy.6 = f32[2048,512]{1,0:T(8,128)} copy(f32[2048,512]{1,0:T(8,128)} %block_products.1) | data formatting | bytes 8388608

commit v3 on v2

--- a/solution.py
+++ b/solution.py
@@ -15,6 +15,7 @@
 FINE = 64.0
 PIECES = 4
 AHEAD = 2
+LEAD = 3
 FIRST, END, SECOND = 1, 2, 3
 
 def lanes_expanded(flags, width, across=1):
@@ -75,6 +76,7 @@
 
     barrier = pltpu.get_barrier_semaphore()
     near = [(-2, 4 * side), (2, -4 * side), (-2, 0), (2, 0), (4, 0), (-1, 3), (-1, -1), (1, -3), (1, 1), (1, -1), (-1, 1)]
+    near += [(4, 2 - 4 * side), (2, 2 - 4 * side), (-2, 2 - 4 * side), (1, 3), (-1, -3), (-1, 5), (1, -5)]
     near += [(0, d) for d in (-3, -2, -1, 1, 2, 3)]
     for di, dj in near:
         pl.semaphore_signal(barrier, inc=1, device_id=at(di, dj), device_id_type=MESH)
@@ -136,11 +138,14 @@
         to = either(at(1, -1), at(-1, 1))
         return remote(place(n, u, Y), place(n, u, Z), send_r.at[Z, n, u], recv_r.at[Z, n, u], to)
 
+    def aside(u):
+        return 2 - 4 * side if u % 2 else 0
+
     def send_too(n, u):
         first = i == 1
         half = jnp.where(first, half_for(1), half_for(3))
-        across = jnp.where(even, 4 * side, 0)
-        to = tuple(jnp.where(first, p, q) for p, q in zip(at(4, 0), at(-2, across), strict=True))
+        across = jnp.where(even, 4 * side, aside(u))
+        to = tuple(jnp.where(first, p, q) for p, q in zip(at(4, jnp.where(even, aside(u), 0)), at(-2, across), strict=True))
         return remote(piece(n, u, half), passing_too(n, u), send_r.at[TOO, n, u], recv_r.at[TOO, n, u], to)
 
     def pass_too(n, u):
@@ -148,8 +153,8 @@
 
     def hand_too(n, u, slot):
         first = i == n_row - 1
-        back = at(-1, 3 - jnp.where(even, 4 * side, 0))
-        to = tuple(jnp.where(first, p, q) for p, q in zip(at(1, 1), back, strict=True))
+        back = at(-1, 3 + jnp.where(even, -4 * side, aside(u)))
+        to = tuple(jnp.where(first, p, q) for p, q in zip(at(1, 1 + jnp.where(even, aside(u), 0)), back, strict=True))
         return remote(passing_too(n, u), place(n, u, slot), send_r.at[EXTRA, n, u], recv_r.at[slot, n, u], to)
 
     gives_x = jnp.where(even, i != 0, i != n_row - 1)
@@ -160,9 +165,20 @@
     def begin(n, u):
         send_via(n, u).start()
 
-        @pl.when(sends_too)
+        @pl.when(i == 2)
         def _():
             send_too(n, u).start()
+
+    def begin_too(n, u):
+        @pl.when(i == 1)
+        def _():
+            send_too(n, u).start()
+
+    def go_on_too(n, u):
+        @pl.when(i == 5)
+        def _():
+            send_too(n, u).wait_recv()
+            pass_too(n, u).start()
 
     def hand_on(n, u):
         send_via(n, u).wait_recv()
@@ -172,20 +188,15 @@
         def _():
             hand_x(n, u).start()
 
-        @pl.when(i == 5)
+        @pl.when(jnp.logical_or(i == 0, i == n_row - 1))
         def _():
             send_too(n, u).wait_recv()
-            pass_too(n, u).start()
-
-        @pl.when(i == 0)
-        def _():
-            send_too(n, u).wait_recv()
-
-        @pl.when(jnp.logical_and(even, i == 0))
+
+        @pl.when(jnp.where(even, i == 0, i == n_row - 1))
         def _():
             hand_too(n, u, X).start()
 
-        @pl.when(jnp.logical_and(other, i == 0))
+        @pl.when(jnp.where(even, i == n_row - 1, i == 0))
         def _():
             hand_too(n, u, Z).start()
 
@@ -195,18 +206,6 @@
         @pl.when(gives_z)
         def _():
             hand_z(n, u).start()
-
-        @pl.when(i == n_row - 1)
-        def _():
-            send_too(n, u).wait_recv()
-
-        @pl.when(jnp.logical_and(even, i == n_row - 1))
-        def _():
-            hand_too(n, u, Z).start()
-
-        @pl.when(jnp.logical_and(other, i == n_row - 1))
-        def _():
-            hand_too(n, u, X).start()
 
     def own_copy(n):
         return pltpu.make_async_copy(block(n, own), held.at[n, :, pl.ds(0, CHUNK)], own_sem.at[n])
@@ -220,11 +219,15 @@
     pl.semaphore_wait(barrier, len(near))
     for u in range(AHEAD):
         begin(0, u)
+    for u in range(min(AHEAD + LEAD, PIECES)):
+        begin_too(0, u)
     own_copy(0).start()
     for n in range(1, chunks):
         load_b(n).wait()
         mask_b(n)
         own_copy(n).start()
+        for u in range(min(AHEAD + LEAD - n * PIECES, PIECES)):
+            begin_too(n, u)
 
     fa[...] = lanes_expanded(af_ref[...], depth)
     size_a = rows // fa.shape[0]
@@ -252,6 +255,9 @@
 
     def z_copy(n, m):
         return remote(zs.at[n, m], zr.at[n, m], send_z.at[n, m], recv_z.at[n, m], either(at(0, -3), at(0, -1)))
+
+    for u in range(LEAD):
+        go_on_too(u // PIECES, u % PIECES)
 
     def product(n, m, first):
         part = pl.ds(pl.multiple_of(m * TILE, TILE), TILE)
@@ -295,6 +301,18 @@
             @pl.when(n + ahead < chunks)
             def _():
                 begin(n + ahead, rest)
+
+            later, rest_later = divmod(u + AHEAD + LEAD, PIECES)
+
+            @pl.when(n + later < chunks)
+            def _():
+                begin_too(n + later, rest_later)
+
+            soon, rest_soon = divmod(u + LEAD, PIECES)
+
+            @pl.when(n + soon < chunks)
+            def _():
+                go_on_too(n + soon, rest_soon)
 
             hand_on(n, u)
             if u == 0:

time: 167 us -> 160 us (0.958); the launches traced: 167 us -> 158 us
  Pallas kernels: 162 us -> 154 us
    pallas_call x1, Pallas kernels: 162 us -> 154 us  [per_device(): pl.pallas_call(functools.partial(kernel, n_row, n_col), name='block_produ...]
where the time goes in v3:
time: 160 us; the launch traced here: 158 us
  Pallas kernels  154 us (96%)
  local copies, waits for them, and re-layouts  4.64 us (3%)
    pallas_call x1, Pallas kernels, per_device(): pl.pallas_call(functools.partial(kernel, n_row, n_col), name='block_produ...  154 us
    unnamed x1, local copies, waits for them, and re-layouts  4.64 us

profile of v3, /device:TPU:1, one launch (start us, length us, event | category | flops | bytes accessed | tf_op | source)
XLA Modules:
  0.0 158.4 jit_solution(16518758066374788462)
XLA Ops:
  0.0 153.7 %block_products.1 = f32[2048,512]{1,0:T(8,128)} custom-call(bf16[2048,2048]{1,0:T(8,128)(2,1)} %a_ref.1, s32[32,32]{1,0:T(8,128)} %af_ref.1, bf16[4096,512]{1,0:T(8,128)(2,1)} %b_ref.1, s32[8,64]{1,0:T(8,128)} %bitcast.1), custom_call_target="tpu_custom_call" | custom-call | flops 17179869184 | bytes 16777216 | tf_op jit(solution)/shard_map/block_products/pallas_call | solution.py:397
  153.7 4.6 %copy.6 = f32[2048,512]{1,0:T(8,128)} copy(f32[2048,512]{1,0:T(8,128)} %block_products.1) | data formatting | bytes 8388608

commit v4 on v3

--- a/solution.py
+++ b/solution.py
@@ -16,7 +16,6 @@
 PIECES = 4
 AHEAD = 2
 LEAD = 3
-FIRST, END, SECOND = 1, 2, 3
 
 def lanes_expanded(flags, width, across=1):
     count = flags.shape[across]
@@ -264,29 +263,33 @@
         pair = held[n, :, first * CHUNK : (first + 2) * CHUNK]
         return jnp.dot(left[part, :], pair, preferred_element_type=jnp.float32)
 
-    def first_pair(n):
-        for u in range(PIECES):
-            hand_x(n, u).wait_recv()
-
-        @pl.loop(0, tiles)
+    half_tiles = tiles // 2
+
+    def first_pair(n, low, high):
+        if low == 0:
+            for u in range(PIECES):
+                hand_x(n, u).wait_recv()
+
+        @pl.loop(low, high)
         def _(m):
             value = product(n, m, X)
             xs[n, m] = value[:, :CHUNK]
             x_copy(n, m).start()
             kept[m] = value[:, CHUNK:]
 
-    def first_end(n):
-        @pl.loop(0, tiles)
+    def first_end(n, low, high):
+        @pl.loop(low, high)
         def _(m):
             x_copy(n, m).wait_recv()
             coded(kept[m] + xr[n, m], qs.at[n, m])
             q_copy(n, m).start()
 
-    def second_pair(n):
-        for u in range(PIECES):
-            hand_z(n, u).wait_recv()
-
-        @pl.loop(0, tiles)
+    def second_pair(n, low, high):
+        if low == 0:
+            for u in range(PIECES):
+                hand_z(n, u).wait_recv()
+
+        @pl.loop(low, high)
         def _(m):
             value = product(n, m, OWN)
             acc[n, m] = value[:, :CHUNK]
@@ -321,23 +324,30 @@
                     hand_third(n - 1, PIECES - 1)
             else:
                 hand_third(n, u - 1)
-            if u == FIRST:
+            if u == 0:
+                @pl.when(n > 1)
+                def _():
+                    second_pair(n - 2, half_tiles, tiles)
+            if u == 1:
                 @pl.when(n > 0)
                 def _():
-                    first_pair(n - 1)
-            if u == END:
+                    first_pair(n - 1, 0, half_tiles)
+            if u == 2:
                 @pl.when(n > 0)
                 def _():
-                    first_end(n - 1)
-            if u == SECOND:
+                    first_pair(n - 1, half_tiles, tiles)
+                    first_end(n - 1, 0, half_tiles)
+            if u == 3:
                 @pl.when(n > 0)
                 def _():
-                    second_pair(n - 1)
+                    first_end(n - 1, half_tiles, tiles)
+                    second_pair(n - 1, 0, half_tiles)
 
     hand_third(chunks - 1, PIECES - 1)
-    first_pair(chunks - 1)
-    first_end(chunks - 1)
-    second_pair(chunks - 1)
+    second_pair(chunks - 2, half_tiles, tiles)
+    first_pair(chunks - 1, 0, tiles)
+    first_end(chunks - 1, 0, tiles)
+    second_pair(chunks - 1, 0, tiles)
 
     def store(n, m):
         where = o_ref.at[

time: 160 us -> 162 us (1.012)
  Pallas kernels: 154 us -> 157 us
    pallas_call x1, Pallas kernels: 154 us -> 157 us  [per_device(): pl.pallas_call(functools.partial(kernel, n_row, n_col), name='block_produ...]
where the time goes in v4:
time: 162 us
  Pallas kernels  157 us (97%)
  local copies, waits for them, and re-layouts  4.64 us (3%)
    pallas_call x1, Pallas kernels, per_device(): pl.pallas_call(functools.partial(kernel, n_row, n_col), name='block_produ...  157 us
    unnamed x1, local copies, waits for them, and re-layouts  4.64 us

profile of v4, /device:TPU:1, one launch (start us, length us, event | category | flops | bytes accessed | tf_op | source)
XLA Modules:
  0.0 161.9 jit_solution(16833476653680255504)
XLA Ops:
  0.0 157.2 %block_products.1 = f32[2048,512]{1,0:T(8,128)} custom-call(bf16[2048,2048]{1,0:T(8,128)(2,1)} %a_ref.1, s32[32,32]{1,0:T(8,128)} %af_ref.1, bf16[4096,512]{1,0:T(8,128)(2,1)} %b_ref.1, s32[8,64]{1,0:T(8,128)} %bitcast.1), custom_call_target="tpu_custom_call" | custom-call | flops 17179869184 | bytes 16777216 | tf_op jit(solution)/shard_map/block_products/pallas_call | solution.py:407
  157.3 4.6 %copy.6 = f32[2048,512]{1,0:T(8,128)} copy(f32[2048,512]{1,0:T(8,128)} %block_products.1) | data formatting | bytes 8388608
